TPU v7x, 32 devices: a whole 2x2x4 slice. The times are simulated.
32 devices in a mesh: seq: 8 (over z, y), item: 4 (over x, core).
Axes of the slice: x: 2, y: 2, z: 4, core: 2. Of those that a mesh axis runs over, the one named last changes fastest.
Arguments:
- inputs: float32 [1024, 24, 768], P('seq', 'item'), may hold values from -6 to 6
- w_in: float32 [768, 3072], replicated, may hold values from -0.21875 to 0.21875
- c_in: float32 [3072], replicated, may hold values from -3 to 3
- w_out: float32 [3072, 768], replicated, may hold values from -0.109375 to 0.109375
- c_out: float32 [768], replicated, may hold values from -3 to 3
- gain_mix: float32 [768], replicated, may hold values from 0.5 to 1.5
- bias_mix: float32 [768], replicated, may hold values from -3 to 3
- gain_out: float32 [768], replicated, may hold values from 0.5 to 1.5
- bias_out: float32 [768], replicated, may hold values from -3 to 3
- cotangent: float32 [1024, 24, 768], P('seq', 'item'), may hold values from -6 to 6
Outputs:
- output: float32 [1024, 24, 768], P('seq', 'item')
- grad_inputs: float32 [1024, 24, 768], P('seq', 'item')
- grad_w_in: float32 [768, 3072], P('seq')
- grad_c_in: float32 [3072], P('seq')
- grad_w_out: float32 [3072, 768], P('seq')
- grad_c_out: float32 [768], P('seq')
- grad_gain_mix: float32 [768], P('seq')
- grad_bias_mix: float32 [768], P('seq')
- grad_gain_out: float32 [768], P('seq')
- grad_bias_out: float32 [768], P('seq')
All inputs are finite; a program needn't handle non-finite values.
Results may differ from a plain program's by a relative error of at most 0.015.
Values may be sent and summed in bfloat16 or wider, within the bound.
A program may use at most 256 MiB of HBM per device.

v0:
```python
import math

import jax
import jax.numpy as jnp
import numpy as np
from jax import lax
from jax.experimental import pallas as pl
from jax.experimental.pallas import tpu as pltpu
from jax.sharding import PartitionSpec as P


def table_block(row_ids, col_ids, period):
    products = row_ids[:, None] * col_ids[None, :] % period
    angles = products.astype(jnp.float32) * (2.0 * math.pi / period)
    return (jnp.cos(angles).astype(jnp.bfloat16), jnp.sin(angles).astype(jnp.bfloat16))


def plain_dot(left, right):
    return jnp.dot(left, right, preferred_element_type=jnp.float32)


def rows_dot(left, right):
    return lax.dot_general(
        left, right, (((0,), (0,)), ((), ())), preferred_element_type=jnp.float32
    )


def cols_dot(left, right):
    return lax.dot_general(
        left, right, (((1,), (1,)), ((), ())), preferred_element_type=jnp.float32
    )


def layer_norm(values, scales, shifts):
    average = jnp.mean(values, axis=-1, keepdims=True)
    centered = values - average
    variance = jnp.mean(centered * centered, axis=-1, keepdims=True)
    return centered * lax.rsqrt(variance + 1e-05) * scales + shifts


def gelu_exact(values):
    return jax.nn.gelu(values, approximate=False)


def gather_body(inputs, w_in, c_in, w_out, c_out, gain_mix, bias_mix, gain_out, bias_out, cotangent):
    local_len, per_dev, features = inputs.shape
    merged = per_dev * features
    period = local_len * lax.axis_size("seq")
    unit_scale = 1.0 / math.sqrt(period * features)
    own_rows = lax.axis_index("seq") * local_len + jnp.arange(local_len, dtype=jnp.int32)
    feat_ids = jnp.arange(features, dtype=jnp.int32)
    cos_hid, sin_hid = table_block(feat_ids, feat_ids, features)
    tokens = inputs.reshape(-1, features)
    tokens_low = tokens.astype(jnp.bfloat16)
    cos_part = (
        plain_dot(tokens_low, cos_hid).astype(jnp.bfloat16).reshape(local_len, per_dev, features)
    )
    sin_part = (
        plain_dot(tokens_low, sin_hid).astype(jnp.bfloat16).reshape(local_len, per_dev, features)
    )
    pieces = (
        lax.all_gather(cos_part, "seq", axis=0, tiled=True),
        lax.all_gather(sin_part, "seq", axis=0, tiled=True),
    )
    col_ids = jnp.arange(pieces[0].shape[0], dtype=jnp.int32)
    cos_blk, sin_blk = table_block(own_rows, col_ids, period)
    mixed = plain_dot(cos_blk, pieces[0].reshape(pieces[0].shape[0], -1)) - plain_dot(
        sin_blk, pieces[1].reshape(pieces[1].shape[0], -1)
    )
    mixed = (mixed * unit_scale).reshape(-1, features)
    hidden, pull_mix = jax.vjp(layer_norm, tokens + mixed, gain_mix, bias_mix)
    hidden_low = hidden.astype(jnp.bfloat16)
    w_in_low = w_in.astype(jnp.bfloat16)
    w_out_low = w_out.astype(jnp.bfloat16)
    pre = plain_dot(hidden_low, w_in_low) + c_in
    act, pull_gelu = jax.vjp(gelu_exact, pre)
    act_low = act.astype(jnp.bfloat16)
    branch = plain_dot(act_low, w_out_low) + c_out
    output, pull_out = jax.vjp(layer_norm, hidden + branch, gain_out, bias_out)
    g_sum2, grad_gain_out, grad_bias_out = pull_out(cotangent.reshape(-1, features))
    g_branch = g_sum2.astype(jnp.bfloat16)
    grad_c_out = jnp.sum(g_branch.astype(jnp.float32), axis=0)
    grad_w_out = rows_dot(act_low, g_branch)
    (g_act,) = pull_gelu(cols_dot(g_branch, w_out_low))
    g_pre = g_act.astype(jnp.bfloat16)
    grad_c_in = jnp.sum(g_pre.astype(jnp.float32), axis=0)
    grad_w_in = rows_dot(hidden_low, g_pre)
    g_hidden = g_sum2 + cols_dot(g_pre, w_in_low)
    g_sum1, grad_gain_mix, grad_bias_mix = pull_mix(g_hidden)
    g_mixed = g_sum1.astype(jnp.bfloat16).reshape(local_len, per_dev, features)
    empty = jnp.zeros((local_len, merged), jnp.float32)
    piece = lax.all_gather(g_mixed, "seq", axis=0, tiled=True)
    row_ids = jnp.arange(piece.shape[0], dtype=jnp.int32)
    cos_blk, sin_blk = table_block(row_ids, own_rows, period)
    flat = piece.reshape(piece.shape[0], -1)
    cycle_gc = rows_dot(cos_blk, flat)
    cycle_gs = (empty, empty)[1] - rows_dot(sin_blk, flat)
    g_cos = (cycle_gc * unit_scale).astype(jnp.bfloat16).reshape(-1, features)
    g_sin = (cycle_gs * unit_scale).astype(jnp.bfloat16).reshape(-1, features)
    grad_inputs = g_sum1 + cols_dot(g_cos, cos_hid) + cols_dot(g_sin, sin_hid)
    shards = (
        lax.psum_scatter(
            grad_w_in.astype(jnp.bfloat16), "seq", scatter_dimension=0, tiled=True
        ).astype(jnp.float32),
        lax.psum_scatter(
            grad_c_in.astype(jnp.bfloat16), "seq", scatter_dimension=0, tiled=True
        ).astype(jnp.float32),
        lax.psum_scatter(
            grad_w_out.astype(jnp.bfloat16), "seq", scatter_dimension=0, tiled=True
        ).astype(jnp.float32),
        lax.psum_scatter(
            grad_c_out.astype(jnp.bfloat16), "seq", scatter_dimension=0, tiled=True
        ).astype(jnp.float32),
        lax.psum_scatter(
            grad_gain_mix.astype(jnp.bfloat16), "seq", scatter_dimension=0, tiled=True
        ).astype(jnp.float32),
        lax.psum_scatter(
            grad_bias_mix.astype(jnp.bfloat16), "seq", scatter_dimension=0, tiled=True
        ).astype(jnp.float32),
        lax.psum_scatter(
            grad_gain_out.astype(jnp.bfloat16), "seq", scatter_dimension=0, tiled=True
        ).astype(jnp.float32),
        lax.psum_scatter(
            grad_bias_out.astype(jnp.bfloat16), "seq", scatter_dimension=0, tiled=True
        ).astype(jnp.float32),
    )
    summed = (
        lax.psum(shards[0].astype(jnp.bfloat16), "item").astype(jnp.float32),
        lax.psum(shards[1].astype(jnp.bfloat16), "item").astype(jnp.float32),
        lax.psum(shards[2].astype(jnp.bfloat16), "item").astype(jnp.float32),
        lax.psum(shards[3].astype(jnp.bfloat16), "item").astype(jnp.float32),
        lax.psum(shards[4].astype(jnp.bfloat16), "item").astype(jnp.float32),
        lax.psum(shards[5].astype(jnp.bfloat16), "item").astype(jnp.float32),
        lax.psum(shards[6].astype(jnp.bfloat16), "item").astype(jnp.float32),
        lax.psum(shards[7].astype(jnp.bfloat16), "item").astype(jnp.float32),
    )
    return (
        output.reshape(inputs.shape),
        grad_inputs.reshape(inputs.shape),
        summed[0],
        summed[1],
        summed[2],
        summed[3],
        summed[4],
        summed[5],
        summed[6],
        summed[7],
    )


def packed_tables(features, parts):
    half = features // 2
    share = half // parts
    index = np.arange(features)
    forward = np.zeros((features, features), np.float32)
    unpack = np.zeros((features, features), np.float32)
    for low in range(half):
        block, place = divmod(low, share)
        cos_slot = block * 2 * share + place
        sin_slot = cos_slot + share
        angles = (index * low % features).astype(np.float32) * np.float32(2.0 * math.pi / features)
        forward[cos_slot] = np.cos(angles)
        unpack[cos_slot, low] = 1.0
        if low:
            unpack[cos_slot, features - low] = 1.0
            forward[sin_slot] = np.sin(angles)
            unpack[sin_slot, low] = -1.0
            unpack[sin_slot, features - low] = 1.0
        else:
            forward[sin_slot] = 1.0 - 2.0 * (index % 2)
            unpack[sin_slot, half] = 1.0
    return forward.astype(jnp.bfloat16), unpack.astype(jnp.bfloat16)


def seq_tables(period):
    index = np.arange(period)
    angles = (index[:, None] * index[None, :] % period).astype(np.float32)
    angles = angles * np.float32(2.0 * math.pi / period)
    return np.cos(angles).astype(jnp.bfloat16), np.sin(angles).astype(jnp.bfloat16)


MESH = pl.DeviceIdType.MESH
CHUNKS = 3
BF16, F32 = jnp.bfloat16, jnp.float32


def dot(left, right, left_dim, right_dim):
    return lax.dot_general(
        left, right, (((left_dim,), (right_dim,)), ((), ())), preferred_element_type=F32
    )


def row_mean(values):
    return jnp.mean(values, axis=-1, keepdims=True)


def layer_kernel(
    x_hbm, cot_hbm, win_hbm, wout_hbm, cin_ref, cout_ref, gmix_ref, bmix_ref, gout_ref, bout_ref,
    fwd_hbm, unp_hbm, cos_hbm, sin_hbm,
    out_hbm, gin_hbm, gmat_ref, gvec_ref,
    fwd_v, unp_v, cos_v, sin_v, prm_v, xbuf, cotb, win_v, wout_v, stage,
    ysend, yrecv, zsend, zrecv, actb, gpb, hb, gbb, dgb, acc, r1b, ostage, vacc,
    recv1, hop0, hop1, hop2, hop3, vsend, vrecv, vmid, vlast,
    ld_sem, x_sem, cot_sem, stg_sem, a_send, a_recv, b_send, b_recv, out_sem,
    core_send, core_recv, red_send, red_recv, gat_send, gat_recv, v_send, v_recv,
):
    chunks, rows, features = xbuf.shape
    per_chunk, share, period = yrecv.shape[2], yrecv.shape[3], yrecv.shape[4]
    own_len = period // 8
    half = share // 2
    unit_scale = 1.0 / math.sqrt(period * features)

    me, item = lax.axis_index("seq"), lax.axis_index("item")
    peers = [(lax.rem(me + k, 8), item) for k in range(1, 8)]
    z_lo, y_at = lax.rem(lax.div(me, 2), 2), lax.rem(me, 2)
    z_at, z_hi = lax.div(me, 2), lax.div(me, 4)
    core, x_at = lax.rem(item, 2), lax.div(item, 2)
    core_peer = (me, item + 1 - 2 * core)
    x_peer = (me, item + 2 - 4 * x_at)
    far_peer = (me, lax.rem(item + 2, 4) + 1 - 2 * core)
    y_peer = (me + 1 - 2 * y_at, item)
    za_peer = (me + 2 - 4 * z_lo, item)
    zb_peer = (me + 4 - 8 * z_hi, item)

    def remote(src, dst, send, recv, peer):
        return pltpu.make_async_remote_copy(
            src_ref=src, dst_ref=dst, send_sem=send, recv_sem=recv, device_id=peer, device_id_type=MESH
        )

    def wait_bytes(ref, sem):
        pltpu.make_async_copy(ref, ref, sem).wait()

    tables = [
        pltpu.make_async_copy(src, dst, ld_sem.at[i])
        for i, (src, dst) in enumerate(
            [(fwd_hbm, fwd_v), (cos_hbm, cos_v), (sin_hbm, sin_v), (unp_hbm, unp_v)]
        )
    ]
    x_loads = [pltpu.make_async_copy(x_hbm.at[c], xbuf.at[c], x_sem.at[c]) for c in range(chunks)]

    def cot_load(c):
        return pltpu.make_async_copy(cot_hbm.at[c], cotb.at[c], cot_sem.at[c])

    x_loads[0].start()
    tables[0].start()
    for load in x_loads[1:] + tables[1:]:
        load.start()

    barrier = pltpu.get_barrier_semaphore()
    everyone = peers + [core_peer, x_peer, far_peer]
    for peer in everyone:
        pl.semaphore_signal(barrier, inc=1, device_id=peer, device_id_type=MESH)

    slots, piece = stage.shape[0], stage.shape[1]
    per_block = features // piece
    steps = 8 * per_block

    def weight_load(step, part, slot):
        block, at = lax.div(step, per_block), lax.rem(step, per_block) * piece
        if part == 0:
            cols = pl.ds(pl.multiple_of(block * features, features), features)
            src = win_hbm.at[pl.ds(pl.multiple_of(at, piece), piece), cols]
        else:
            src = wout_hbm.at[pl.ds(pl.multiple_of(block * features + at, piece), piece), :]
        return pltpu.make_async_copy(src, stage.at[slot], stg_sem.at[slot])

    def cast_weights(part):
        total = 4 * per_block
        groups = piece // share

        def one(step, carry):
            slot = lax.rem(step, slots)
            weight_load(step, part, slot).wait()
            block, at = lax.div(step, per_block), lax.rem(step, per_block) * groups
            value = stage[slot].astype(BF16)
            for g in range(groups):
                where = at + g
                rows_of = value[g * share : (g + 1) * share]
                if part == 0:
                    win_v[block, lax.div(where, 2), lax.rem(where, 2)] = rows_of
                else:
                    wout_v[block, lax.div(where, 4), lax.rem(lax.div(where, 2), 2), lax.rem(where, 2)] = rows_of

            @pl.when(step + slots < total)
            def _():
                weight_load(step + slots, part, slot).start()

            return carry

        lax.fori_loop(0, total, one, 0)

    def first_loads(part):
        for slot in range(slots):
            weight_load(jnp.int32(slot), part, jnp.int32(slot)).start()

    def in_block(j):
        return win_v[j].reshape(features, features)

    def out_block(j):
        return wout_v[j].reshape(features, features)

    def pack(c, low):
        packed = dot(fwd_v[...], low, 1, 1).astype(BF16)
        for s in range(per_chunk):
            ysend[c, s] = packed[:, s * own_len : (s + 1) * own_len]

    def send_owners(way, c):
        mine = pl.ds(pl.multiple_of(me * own_len, own_len), own_len)
        for peer in peers:
            to = pl.ds(pl.multiple_of(peer[0] * share, share), share)
            remote(
                ysend.at[c, :, to, :], yrecv.at[way, c, :, :, mine], a_send.at[way, c], a_recv.at[way, c], peer
            ).start()
        own = pl.ds(pl.multiple_of(me * share, share), share)
        pltpu.make_async_copy(ysend.at[c, :, own, :], yrecv.at[way, c, :, :, mine], a_recv.at[way, c]).start()

    def owners_sent(way, c):
        wait_bytes(ysend.at[c, :, pl.ds(0, 7 * share), :], a_send.at[way, c])

    def turn(way, c):
        wait_bytes(yrecv.at[way, c], a_recv.at[way, c])
        held = yrecv[way, c]
        cos_rows = held[:, :half].reshape(per_chunk * half, period)
        sin_rows = held[:, half:].reshape(per_chunk * half, period)
        mid_rows = held[:, half : half + 16].reshape(per_chunk * 16, period)
        wide = period // 4
        top = lax.broadcasted_iota(jnp.int32, (16, wide), 0) == 0
        top = jnp.logical_and(top, me == 0)
        cos_rows = jnp.concatenate([cos_rows, mid_rows], axis=0)

        def one(n, carry):
            cols = pl.ds(pl.multiple_of(n * wide, wide), wide)
            by_cos = dot(cos_rows, cos_v[:, cols], 1, 0) * unit_scale
            by_sin = dot(sin_rows, sin_v[:, cols], 1, 0) * unit_scale
            for s in range(per_chunk):
                zsend[c, s, :half, cols] = by_cos[s * half : (s + 1) * half].astype(BF16)
                sin_part = by_sin[s * half : (s + 1) * half]
                at = per_chunk * half + s * 16
                zsend[c, s, half : half + 16, cols] = jnp.where(top, by_cos[at : at + 16], sin_part[:16]).astype(BF16)
                zsend[c, s, half + 16 :, cols] = sin_part[16:].astype(BF16)
            return carry

        lax.fori_loop(0, 4, one, 0)

    def send_back(way, c):
        mine = pl.ds(pl.multiple_of(me * share, share), share)
        for peer in peers:
            to = pl.ds(pl.multiple_of(peer[0] * own_len, own_len), own_len)
            remote(
                zsend.at[c, :, :, to], zrecv.at[c, :, mine, :], b_send.at[way, c], b_recv.at[way, c], peer
            ).start()
        own = pl.ds(pl.multiple_of(me * own_len, own_len), own_len)
        pltpu.make_async_copy(zsend.at[c, :, :, own], zrecv.at[c, :, mine, :], b_recv.at[way, c]).start()

    def return_sent(way, c):
        wait_bytes(zsend.at[c, :, :, pl.ds(0, 7 * own_len)], b_send.at[way, c])

    def mixed_of(c, way=0):
        wait_bytes(zrecv.at[c], b_recv.at[way, c])
        held = jnp.concatenate([zrecv[c, s] for s in range(per_chunk)], axis=1)
        return dot(held, unp_v[...], 0, 0)

    tables[0].wait()
    x_loads[0].wait()
    first_loads(0)
    pack(0, xbuf[0].astype(BF16))
    pl.semaphore_wait(barrier, len(everyone))
    send_owners(0, 0)
    x_loads[1].wait()
    pack(1, xbuf[1].astype(BF16))
    for c in range(chunks):
        cot_load(c).start()
    vacc[...] = jnp.zeros_like(vacc)
    for j in range(4):
        prm_v[j : j + 1] = cin_ref[j * features : (j + 1) * features].reshape(1, features)
    for r, ref in enumerate((cout_ref, gmix_ref, bmix_ref, gout_ref, bout_ref)):
        prm_v[4 + r : 5 + r] = ref[...].reshape(1, features)
    cast_weights(0)
    first_loads(1)
    send_owners(0, 1)
    x_loads[2].wait()
    pack(2, xbuf[2].astype(BF16))
    cast_weights(1)
    for load in tables[1:]:
        load.wait()
    turn(0, 0)
    send_back(0, 0)
    owners_sent(0, 0)
    owners_sent(0, 1)
    send_owners(0, 2)
    turn(0, 1)

    gain_mix, bias_mix = prm_v[5:6], prm_v[6:7]
    gain_out, bias_out, c_out = prm_v[7:8], prm_v[8:9], prm_v[4:5]

    def out_copy(c):
        return pltpu.make_async_copy(ostage, out_hbm.at[c], out_sem.at[0])

    def feed_up(c, mixed=None):
        value = xbuf[c] + (mixed_of(c) if mixed is None else mixed)
        value = value - row_mean(value)
        scale = lax.rsqrt(row_mean(value * value) + 1e-05)
        normal = value * scale
        r1b[...] = jnp.broadcast_to(scale, r1b.shape)
        xbuf[c] = normal
        hidden = normal * gain_mix + bias_mix
        hb[c] = hidden.astype(BF16)
        acc[...] = hidden + c_out

        def up(j, carry):
            pre = dot(hb[c], in_block(j), 1, 0) + prm_v[pl.ds(j, 1)]
            prob = 0.5 + 0.5 * lax.erf(pre * math.sqrt(0.5))
            density = jnp.exp(-0.5 * pre * pre) * (1.0 / math.sqrt(2.0 * math.pi))
            act = (pre * prob).astype(BF16)
            dgb[j] = prob + pre * density
            actb[j, c] = act
            acc[...] += dot(act, out_block(j), 1, 0)
            return carry

        lax.fori_loop(0, 4, up, 0, unroll=True)

    def feed_mid(c):
        value = acc[...]
        value = value - row_mean(value)
        scale = lax.rsqrt(row_mean(value * value) + 1e-05)
        normal = value * scale


        @pl.when(c > 0)
        def _():
            out_copy(c - 1).wait()

        ostage[...] = (normal * gain_out + bias_out).astype(BF16)
        out_copy(c).start()
        cot_load(c).wait()
        cot = cotb[c]
        vacc[7:8] += jnp.sum(cot * normal, axis=0, keepdims=True)
        vacc[8:9] += jnp.sum(cot, axis=0, keepdims=True)
        scaled = cot * gain_out
        g_sum2 = scale * (scaled - row_mean(scaled) - normal * row_mean(scaled * normal))
        low = g_sum2.astype(BF16)
        gbb[c] = low
        vacc[4:5] += jnp.sum(low.astype(F32), axis=0, keepdims=True)
        acc[...] = g_sum2

    def feed_down(c):
        for j in range(4):
            g_pre = (dot(gbb[c], out_block(j), 1, 1) * dgb[j]).astype(BF16)
            gpb[j, c] = g_pre
            vacc[j : j + 1] += jnp.sum(g_pre.astype(F32), axis=0, keepdims=True)

    def feed_end(c):
        for j in range(4):
            acc[...] += dot(gpb[j, c], in_block(j), 1, 1)
        g_hidden = acc[...]
        normal = xbuf[c]
        vacc[5:6] += jnp.sum(g_hidden * normal, axis=0, keepdims=True)
        vacc[6:7] += jnp.sum(g_hidden, axis=0, keepdims=True)
        scaled = g_hidden * gain_mix
        g_sum1 = r1b[:, :1] * (scaled - row_mean(scaled) - normal * row_mean(scaled * normal))
        xbuf[c] = g_sum1
        pack(c, g_sum1.astype(BF16))

    cut = hop3.shape[3]
    routes = ('xyz', 'xyz', 'yxz', 'xzy', 'yxz', 'xzy')
    z_pair = lax.rem(z_at + 2, 4)
    z_next = z_at + 1 - 2 * z_lo
    z_far = lax.rem(z_next + 2, 4)

    def part(p):
        return pl.ds((p % 3) * cut, cut)

    def add(*terms):
        total = terms[0].astype(F32)
        for term in terms[1:]:
            total = total + term.astype(F32)
        return total.astype(BF16)

    def product(p):
        kind, h, at = p // 3, p % 3, part(p)

        def one_in(i, carry):
            x = lax.rem(i, 2)
            q = jnp.where(i < 2, 2 * x + 1 - core, 2 * x + core)
            grad = dot(hb[...].reshape(-1, features), gpb[q, :, :, at].reshape(-1, cut), 0, 0)
            win_v[q, :, :, :, at] = grad.astype(BF16).reshape(4, 2, share, cut)

            @pl.when(i < 2)
            def _():
                remote(
                    win_v.at[2 * x + 1 - core, :, :, :, at], recv1.at[0, h, x],
                    core_send.at[0, h], core_recv.at[0, h], core_peer,
                ).start()

            return carry

        def one_out(j, carry):
            grad = dot(actb[j].reshape(-1, features), gbb[:, :, at].reshape(-1, cut), 0, 0)
            wout_v[j, :, :, :, :, at] = grad.astype(BF16).reshape(2, 2, 2, share, cut)
            return carry

        if kind == 0:
            lax.fori_loop(0, 4, one_in, 0)
        else:
            lax.fori_loop(0, 4, one_out, 0)
            for x in range(2):
                remote(
                    wout_v.at[:, :, x, 1 - core, :, at], recv1.at[1, h, x], core_send.at[1, h], core_recv.at[1, h], core_peer
                ).start()

    def hop(p, step):
        kind, h, at = p // 3, p % 3, part(p)
        legs = routes[p].replace("z", "ab")
        past = legs[:step]
        grads = (win_v, wout_v)[kind]
        landing = (hop0, hop1, hop2, hop3)
        if step == 0:
            wait_bytes(recv1.at[kind, h], core_recv.at[kind, h])
        else:
            wait_bytes(landing[step - 1].at[p], red_recv.at[step - 1, p])

        def place(x, z, y):
            return (2 * x + core, z, y, slice(None), at) if kind == 0 else (z, y, x, core, slice(None), at)

        def arrived(x, z, y, rows_at=slice(None)):
            if step == 0:
                return recv1[kind, h, x, z, y, rows_at]
            count_z = 1 if "b" in past else 2 if "a" in past else 4
            count_y = 1 if "y" in past else 2
            slot = (0 if "x" in past else x * count_z) + zslot(z)
            if isinstance(y, slice):
                return landing[step - 1][p, pl.ds(slot * 2, 2), rows_at]
            return landing[step - 1][p, slot * count_y + (0 if count_y == 1 else y), rows_at]

        def zslot(z):
            if "a" not in past:
                return z
            return 0 if z is z_at else 1

        both_y = slice(None)
        xs = (x_at,) if "x" in past else (0, 1)
        ys = (y_at,) if "y" in past else (both_y,)
        zs = (z_at,) if "b" in past else (z_at, z_pair) if "a" in past else tuple(range(4))

        def put(x, z, y):
            def rows_of(r, carry):
                rows_at = pl.ds(pl.multiple_of(r * 32, 32), 32)
                where = place(x, z, y)
                where = where[:-2] + (rows_at, at)
                grads[where] = add(grads[where], arrived(x, z, y, rows_at))
                return carry

            lax.fori_loop(0, share // 32, rows_of, 0)

        if step == 4:
            where = place(x_at, z_at, y_at)
            finish(p, add(grads[where], arrived(x_at, z_at, y_at)))
            return
        leg = legs[step]
        if leg == "x":
            away, keep, peer = [(1 - x_at, z, y) for z in zs for y in ys], [(x_at, z, y) for z in zs for y in ys], x_peer
        elif leg == "y":
            away, keep, peer = [(x, z, 1 - y_at) for x in xs for z in zs], [(x, z, y_at) for x in xs for z in zs], y_peer
        elif leg == "a":
            away = [(x, z, y) for x in xs for z in (z_next, z_far) for y in ys]
            keep, peer = [(x, z, y) for x in xs for z in (z_at, z_pair) for y in ys], za_peer
        else:
            away, keep, peer = [(x, z_pair, y) for x in xs for y in ys], [(x, z_at, y) for x in xs for y in ys], zb_peer
        for x, z, y in away:
            put(x, z, y)
        for count, (x, z, y) in enumerate(away):
            width = 2 if isinstance(y, slice) else 1
            dst = landing[step].at[p, pl.ds(count * 2, 2)] if width == 2 else landing[step].at[p, count]
            remote(grads.at[place(x, z, y)], dst, red_send.at[step, p], red_recv.at[step, p], peer).start()
        for x, z, y in keep:
            put(x, z, y)

    def finish(p, total):
        kind, at = p // 3, part(p)
        gmat_ref[kind, item, :, at] = total
        here = gmat_ref.at[kind, item, :, at]
        remote(here, here, gat_send.at[1, p], gat_recv.at[1, p], x_peer).start()
        remote(here, here, gat_send.at[0, p], gat_recv.at[0, p], core_peer).start()
        if p in (2, 3):
            remote(here, here, gat_send.at[2, p], gat_recv.at[2, p], far_peer).start()

    def forward_on(p):
        there = gmat_ref.at[p // 3, x_peer[1], :, part(p)]
        wait_bytes(there, gat_recv.at[1, p])
        if p not in (2, 3):
            remote(there, there, gat_send.at[2, p], gat_recv.at[2, p], core_peer).start()

    def final(c):
        hb[c] = (xbuf[c] + mixed_of(c, 1)).astype(BF16)
        pltpu.make_async_copy(hb.at[c], gin_hbm.at[c], out_sem.at[1]).start()

    def vectors_out():
        lanes = vsend.shape[2]
        vsend[...] = jnp.zeros_like(vsend)
        for d in range(8):
            at = d * (features // 2)
            for r in range(3):
                where = at + r * lanes
                vsend[d, r : r + 1, :] = vacc[where // features : where // features + 1, where % features : where % features + lanes]
            for r in range(5):
                vsend[d, 3 + r : 4 + r, :share] = vacc[4 + r : 5 + r, d * share : (d + 1) * share]
        for peer in peers:
            remote(vsend.at[peer[0]], vrecv.at[me], v_send.at[0], v_recv.at[0], peer).start()
        pltpu.make_async_copy(vsend.at[me], vrecv.at[me], v_recv.at[0]).start()

    def vectors_on():
        wait_bytes(vrecv, v_recv.at[0])
        vmid[...] = jnp.sum(vrecv[...], axis=0)
        remote(vmid, vlast.at[0], v_send.at[1], v_recv.at[1], core_peer).start()

    def vectors_over():
        wait_bytes(vlast.at[0], v_recv.at[1])
        vlast[1] = vmid[...] + vlast[0]
        remote(vlast.at[1], vlast.at[2], v_send.at[2], v_recv.at[2], x_peer).start()

    def vectors_end():
        wait_bytes(vlast.at[2], v_recv.at[2])
        gvec_ref[...] = vlast[1] + vlast[2]

    def feed(c, carry):
        feed_up(c)

        @pl.when(c == 0)
        def _():
            send_back(0, 1)
            owners_sent(0, 2)

        @pl.when(c == 1)
        def _():
            send_owners(1, 0)

        feed_mid(c)

        @pl.when(c == 0)
        def _():
            turn(0, 2)
            send_back(0, 2)

        feed_down(c)

        @pl.when(c == chunks - 1)
        def _():
            product(3)
            return_sent(0, 0)
            turn(1, 0)
            send_back(1, 0)
            hop(3, 0)

        feed_end(c)

        @pl.when(c == 1)
        def _():
            send_owners(1, 1)

        return carry

    lax.fori_loop(0, chunks, feed, 0)
    send_owners(1, 2)
    product(4)
    product(5)
    hop(4, 0)
    hop(5, 0)
    return_sent(0, 1)
    turn(1, 1)
    send_back(1, 1)
    product(1)
    product(0)
    hop(3, 1)
    vectors_out()
    product(2)
    hop(0, 0)
    hop(2, 0)
    hop(5, 1)
    hop(1, 0)
    hop(3, 2)
    hop(0, 1)
    hop(5, 2)
    hop(4, 1)
    return_sent(0, 2)
    turn(1, 2)
    send_back(1, 2)
    final(0)
    hop(2, 1)
    hop(0, 2)
    vectors_on()
    hop(1, 1)
    hop(3, 3)
    hop(4, 2)
    hop(0, 3)
    vectors_over()
    hop(5, 3)
    final(1)
    hop(1, 2)
    hop(3, 4)
    hop(2, 2)
    hop(4, 3)
    hop(5, 4)
    hop(1, 3)
    hop(2, 3)
    hop(0, 4)
    hop(1, 4)
    final(2)
    hop(4, 4)
    hop(2, 4)
    forward_on(0)
    vectors_end()
    forward_on(4)
    forward_on(1)
    forward_on(5)
    forward_on(2)
    forward_on(3)

    out_copy(chunks - 1).wait()
    wait_bytes(hb, out_sem.at[1])
    for c in range(chunks):
        owners_sent(1, c)
        return_sent(1, c)
    for kind in range(2):
        for h in range(3):
            wait_bytes(recv1.at[kind, h], core_send.at[kind, h])
    for p in range(6):
        for step, ref in enumerate((hop0, hop1, hop2, hop3)):
            wait_bytes(ref.at[p], red_send.at[step, p])
        for leg in range(3):
            wait_bytes(hop3.at[p], gat_send.at[leg, p])
        wait_bytes(hop3.at[p], gat_recv.at[0, p])
        wait_bytes(hop3.at[p], gat_recv.at[2, p])
    wait_bytes(vrecv.at[pl.ds(0, 7)], v_send.at[0])
    wait_bytes(vlast.at[1], v_send.at[1])
    wait_bytes(vlast.at[1], v_send.at[2])


def finish_kernel(
    out_in, gin_in, gmat_in, gvec_in,
    out_ref, gin_ref, gwi_ref, gwo_ref, gci_ref, gco_ref, ggm_ref, gbm_ref, ggo_ref, gbo_ref,
    low, mv, res, wi, wo, sem_in, sem_out,
):
    chunks, features, share = low.shape[1], low.shape[3], mv.shape[2]
    loads = [pltpu.make_async_copy(gmat_in, mv, sem_in.at[0])]
    for k, src in enumerate((out_in, gin_in)):
        for c in range(chunks):
            loads.append(pltpu.make_async_copy(src.at[c], low.at[k, c], sem_in.at[len(loads)]))
    for load in loads:
        load.start()
    stores = []

    def put(src, dst):
        copy = pltpu.make_async_copy(src, dst, sem_out.at[len(stores)])
        copy.start()
        stores.append(copy)

    loads[0].wait()
    for q in range(4):
        wi[:, q * features : (q + 1) * features] = mv[0, q].astype(F32)
        wo[q * share : (q + 1) * share] = mv[1, q].astype(F32)
    put(wi, gwi_ref)
    put(wo, gwo_ref)
    for k, dst in enumerate((out_ref, gin_ref)):
        for c in range(chunks):
            loads[1 + k * chunks + c].wait()
            res[k, c] = low[k, c].astype(F32)
            put(res.at[k, c], dst.at[c])
    lanes = gvec_in.shape[1]
    for r in range(3):
        gci_ref[r * lanes : (r + 1) * lanes] = gvec_in[r]
    for r, ref in enumerate((gco_ref, ggm_ref, gbm_ref, ggo_ref, gbo_ref)):
        ref[...] = gvec_in[3 + r, :share]
    for copy in stores:
        copy.wait()


def exchange_body(inputs, w_in, c_in, w_out, c_out, gain_mix, bias_mix, gain_out, bias_out, cotangent):
    local_len, per_dev, features = inputs.shape
    parts = lax.axis_size("seq")
    period = local_len * parts
    share = features // parts
    per_chunk = per_dev // CHUNKS
    rows = per_chunk * local_len
    forward, unpack = packed_tables(features, parts)
    cos_seq, sin_seq = seq_tables(period)
    held = jnp.swapaxes(inputs, 0, 1).reshape(CHUNKS, rows, features)
    cot = jnp.swapaxes(cotangent, 0, 1).reshape(CHUNKS, rows, features)
    anywhere = pl.BlockSpec(memory_space=pl.ANY)
    whole = (CHUNKS, rows, features)
    vm, dma = pltpu.VMEM, pltpu.SemaphoreType.DMA
    inside = pl.BlockSpec(memory_space=pltpu.VMEM)
    out_low, gin_low, mats, vecs = pl.pallas_call(
        layer_kernel,
        out_shape=(
            jax.ShapeDtypeStruct(whole, BF16),
            jax.ShapeDtypeStruct(whole, BF16),
            jax.ShapeDtypeStruct((2, 4, share, features), BF16),
            jax.ShapeDtypeStruct((8, 128), F32),
        ),
        in_specs=[anywhere] * 4 + [inside] * 6 + [anywhere] * 4,
        out_specs=(anywhere, anywhere, inside, inside),
        scratch_shapes=[
            vm((features, features), BF16),
            vm((features, features), BF16),
            vm((period, period), BF16),
            vm((period, period), BF16),
            vm((16, features), F32),
            vm(whole, F32),
            vm(whole, F32),
            vm((4, 4, 2, share, features), BF16),
            vm((4, 2, 2, 2, share, features), BF16),
            vm((4, 192, features), F32),
            vm((CHUNKS, per_chunk, features, local_len), BF16),
            vm((2, CHUNKS, per_chunk, share, period), BF16),
            vm((CHUNKS, per_chunk, share, period), BF16),
            vm((CHUNKS, per_chunk, features, local_len), BF16),
            vm((4,) + whole, BF16),
            vm((4,) + whole, BF16),
            vm(whole, BF16),
            vm(whole, BF16),
            vm((4, rows, features), F32),
            vm((rows, features), F32),
            vm((rows, 128), F32),
            vm((rows, features), BF16),
            vm((16, features), F32),
            vm((2, 3, 2, 4, 2, share, features // 3), BF16),
            vm((6, 8, share, features // 3), BF16),
            vm((6, 4, share, features // 3), BF16),
            vm((6, 2, share, features // 3), BF16),
            vm((6, 1, share, features // 3), BF16),
            vm((8, 8, 128), F32),
            vm((8, 8, 128), F32),
            vm((8, 128), F32),
            vm((3, 8, 128), F32),
            dma((4,)),
            dma((CHUNKS,)),
            dma((CHUNKS,)),
            dma((4,)),
            dma((2, CHUNKS)),
            dma((2, CHUNKS)),
            dma((2, CHUNKS)),
            dma((2, CHUNKS)),
            dma((2,)),
            dma((2, 3)),
            dma((2, 3)),
            dma((4, 6)),
            dma((4, 6)),
            dma((3, 6)),
            dma((3, 6)),
            dma((3,)),
            dma((3,)),
        ],
        compiler_params=pltpu.CompilerParams(
            collective_id=0, has_side_effects=True, vmem_limit_bytes=62 * 1024 * 1024
        ),
    )(held, cot, w_in, w_out, c_in, c_out, gain_mix, bias_mix, gain_out, bias_out, forward, unpack, cos_seq, sin_seq)
    shape = (per_dev, local_len, features)
    vec = lambda n: jax.ShapeDtypeStruct((n,), F32)
    output, grad_inputs, grad_in, grad_out, grad_c_in, *others = pl.pallas_call(
        finish_kernel,
        in_specs=[anywhere] * 3 + [inside],
        out_specs=(anywhere,) * 4 + (inside,) * 6,
        out_shape=(
            jax.ShapeDtypeStruct(whole, F32),
            jax.ShapeDtypeStruct(whole, F32),
            jax.ShapeDtypeStruct((share, 4 * features), F32),
            jax.ShapeDtypeStruct((4 * share, features), F32),
            vec(4 * share),
        )
        + (vec(share),) * 5,
        scratch_shapes=[
            vm((2,) + whole, BF16),
            vm((2, 4, share, features), BF16),
            vm((2,) + whole, F32),
            vm((share, 4 * features), F32),
            vm((4 * share, features), F32),
            dma((1 + 2 * CHUNKS,)),
            dma((2 + 2 * CHUNKS,)),
        ],
        compiler_params=pltpu.CompilerParams(vmem_limit_bytes=60 * 1024 * 1024),
    )(out_low, gin_low, mats, vecs)
    output = jnp.swapaxes(output.reshape(shape), 0, 1)
    grad_inputs = jnp.swapaxes(grad_inputs.reshape(shape), 0, 1)
    return (output, grad_inputs, grad_in, grad_c_in, grad_out, *others)


def body(inputs, *rest):
    if lax.axis_size("seq") != 8 or lax.axis_size("item") != 4:
        return gather_body(inputs, *rest)
    return exchange_body(inputs, *rest)


def solution(mesh):
    placed = (
        P("seq", "item", None),
        P(),
        P(),
        P(),
        P(),
        P(),
        P(),
        P(),
        P(),
        P("seq", "item", None),
    )
    return jax.shard_map(
        body,
        mesh=mesh,
        in_specs=placed,
        out_specs=(
            P("seq", "item", None),
            P("seq", "item", None),
            P("seq", None),
            P("seq"),
            P("seq", None),
            P("seq"),
            P("seq"),
            P("seq"),
            P("seq"),
            P("seq"),
        ),
        check_vma=False,
    )
```

profile of v0, /device:TPU:0, one launch (start us, length us, event | category | flops | bytes accessed | tf_op | source)
XLA Modules:
  0.0 147.8 jit_solution(5501622914619980391)
XLA Ops:
  0.6 141.3 %shard_map.213 = (bf16[3,256,768]{2,1,0:T(8,128)(2,1)}, bf16[3,256,768]{2,1,0:T(8,128)(2,1)}, bf16[2,4,96,768]{3,2,1,0:T(8,128)(2,1)}, f32[8,128]{1,0:T(8,128)}) custom-call(f32[3,256,768]{2,1,0:T(8,128)} %bitcast.12, f32[3,256,768]{2,1,0:T(8,128)} %bitcast.13, f32[768,3072]{1,0:T(8,128)} %win_hbm.1, f32[3072,768]{1,0:T(8,128)} %wout_hbm.1, f32[3072]{0:T(1024)} %cin_ref.1, ...), custom_call_target="tpu_custom_call" | custom-call | tf_op jit(solution)/shard_map/pallas_call | solution.py:792
  142.0 5.6 %shard_map.214 = (f32[3,256,768]{2,1,0:T(8,128)}, f32[3,256,768]{2,1,0:T(8,128)}, f32[96,3072]{1,0:T(8,128)}, f32[384,768]{1,0:T(8,128)}, f32[384]{0:T(512)}, /*...) custom-call(bf16[3,256,768]{2,1,0:T(8,128)(2,1)} %get-tuple-element.24.out_in, ...), custom_call_target="tpu_custom_call" | custom-call | tf_op jit(solution)/shard_map/pallas_call | solution.py:859
where the time goes:
time: 148 us
  Pallas kernels  147 us (99%)
    pallas_call x1, Pallas kernels, exchange_body(): pl.pallas_call(layer_kernel, out_shape=(jax.ShapeDtypeStruct(whole, BF16)...  141 us
    pallas_call x1, Pallas kernels, exchange_body(): pl.pallas_call(finish_kernel, in_specs=[anywhere] * 3 + [inside], out_spe...  5.63 us

commit v1 on v0

--- a/solution.py
+++ b/solution.py
@@ -195,9 +195,10 @@
 
 
 def layer_kernel(
-    x_hbm, cot_hbm, win_hbm, wout_hbm, cin_ref, cout_ref, gmix_ref, bmix_ref, gout_ref, bout_ref,
+    x_hbm, cot_hbm, win_hbm, wout_hbm, cin_hbm, cout_hbm, gmix_hbm, bmix_hbm, gout_hbm, bout_hbm,
     fwd_hbm, unp_hbm, cos_hbm, sin_hbm,
     out_hbm, gin_hbm, gmat_ref, gvec_ref,
+    cin_ref, cout_ref, gmix_ref, bmix_ref, gout_ref, bout_ref,
     fwd_v, unp_v, cos_v, sin_v, prm_v, xbuf, cotb, win_v, wout_v, stage,
     ysend, yrecv, zsend, zrecv, actb, gpb, hb, gbb, dgb, acc, r1b, ostage, vacc,
     recv1, hop0, hop1, hop2, hop3, vsend, vrecv, vmid, vlast,
@@ -233,7 +234,11 @@
     tables = [
         pltpu.make_async_copy(src, dst, ld_sem.at[i])
         for i, (src, dst) in enumerate(
-            [(fwd_hbm, fwd_v), (cos_hbm, cos_v), (sin_hbm, sin_v), (unp_hbm, unp_v)]
+            [
+                (fwd_hbm, fwd_v), (cos_hbm, cos_v), (sin_hbm, sin_v), (unp_hbm, unp_v),
+                (cin_hbm, cin_ref), (cout_hbm, cout_ref), (gmix_hbm, gmix_ref),
+                (bmix_hbm, bmix_ref), (gout_hbm, gout_ref), (bout_hbm, bout_ref),
+            ]
         )
     ]
     x_loads = [pltpu.make_async_copy(x_hbm.at[c], xbuf.at[c], x_sem.at[c]) for c in range(chunks)]
@@ -371,6 +376,8 @@
     for c in range(chunks):
         cot_load(c).start()
     vacc[...] = jnp.zeros_like(vacc)
+    for load in tables[4:]:
+        load.wait()
     for j in range(4):
         prm_v[j : j + 1] = cin_ref[j * features : (j + 1) * features].reshape(1, features)
     for r, ref in enumerate((cout_ref, gmix_ref, bmix_ref, gout_ref, bout_ref)):
@@ -381,7 +388,7 @@
     x_loads[2].wait()
     pack(2, xbuf[2].astype(BF16))
     cast_weights(1)
-    for load in tables[1:]:
+    for load in tables[1:4]:
         load.wait()
     turn(0, 0)
     send_back(0, 0)
@@ -462,7 +469,7 @@
         pack(c, g_sum1.astype(BF16))
 
     cut = hop3.shape[3]
-    routes = ('xyz', 'xyz', 'yxz', 'xzy', 'yxz', 'xzy')
+    routes = ('xyz', 'xzy', 'xyz', 'xzy', 'yxz', 'yxz')
     z_pair = lax.rem(z_at + 2, 4)
     z_next = z_at + 1 - 2 * z_lo
     z_far = lax.rem(z_next + 2, 4)
@@ -581,13 +588,13 @@
         here = gmat_ref.at[kind, item, :, at]
         remote(here, here, gat_send.at[1, p], gat_recv.at[1, p], x_peer).start()
         remote(here, here, gat_send.at[0, p], gat_recv.at[0, p], core_peer).start()
-        if p in (2, 3):
+        if p in (1, 4, 5):
             remote(here, here, gat_send.at[2, p], gat_recv.at[2, p], far_peer).start()
 
     def forward_on(p):
         there = gmat_ref.at[p // 3, x_peer[1], :, part(p)]
         wait_bytes(there, gat_recv.at[1, p])
-        if p not in (2, 3):
+        if p not in (1, 4, 5):
             remote(there, there, gat_send.at[2, p], gat_recv.at[2, p], core_peer).start()
 
     def final(c):
@@ -649,6 +656,7 @@
             return_sent(0, 0)
             turn(1, 0)
             send_back(1, 0)
+            product(4)
             hop(3, 0)
 
         feed_end(c)
@@ -660,60 +668,59 @@
         return carry
 
     lax.fori_loop(0, chunks, feed, 0)
+    vectors_out()
+    hop(4, 0)
     send_owners(1, 2)
-    product(4)
-    product(5)
-    hop(4, 0)
-    hop(5, 0)
+    product(0)
+    product(1)
+    hop(0, 0)
+    hop(1, 0)
+    hop(3, 1)
     return_sent(0, 1)
     turn(1, 1)
     send_back(1, 1)
-    product(1)
-    product(0)
-    hop(3, 1)
-    vectors_out()
     product(2)
-    hop(0, 0)
-    hop(2, 0)
-    hop(5, 1)
-    hop(1, 0)
+    product(5)
     hop(3, 2)
     hop(0, 1)
-    hop(5, 2)
-    hop(4, 1)
+    vectors_on()
+    vectors_over()
+    hop(5, 0)
     return_sent(0, 2)
     turn(1, 2)
     send_back(1, 2)
     final(0)
+    hop(2, 0)
+    hop(4, 1)
+    hop(1, 1)
+    hop(0, 2)
+    hop(5, 1)
     hop(2, 1)
-    hop(0, 2)
-    vectors_on()
-    hop(1, 1)
     hop(3, 3)
+    hop(1, 2)
     hop(4, 2)
     hop(0, 3)
-    vectors_over()
-    hop(5, 3)
+    hop(2, 2)
+    hop(3, 4)
+    hop(5, 2)
+    hop(4, 3)
     final(1)
-    hop(1, 2)
-    hop(3, 4)
-    hop(2, 2)
-    hop(4, 3)
-    hop(5, 4)
     hop(1, 3)
     hop(2, 3)
+    forward_on(3)
     hop(0, 4)
+    hop(5, 3)
     hop(1, 4)
-    final(2)
     hop(4, 4)
     hop(2, 4)
+    hop(5, 4)
+    vectors_end()
+    final(2)
+    forward_on(2)
     forward_on(0)
-    vectors_end()
+    forward_on(1)
     forward_on(4)
-    forward_on(1)
     forward_on(5)
-    forward_on(2)
-    forward_on(3)
 
     out_copy(chunks - 1).wait()
     wait_bytes(hb, out_sem.at[1])
@@ -745,7 +752,7 @@
     for k, src in enumerate((out_in, gin_in)):
         for c in range(chunks):
             loads.append(pltpu.make_async_copy(src.at[c], low.at[k, c], sem_in.at[len(loads)]))
-    for load in loads:
+    for load in loads[1:] + loads[:1]:
         load.start()
     stores = []
 
@@ -754,17 +761,17 @@
         copy.start()
         stores.append(copy)
 
+    for k, dst in enumerate((out_ref, gin_ref)):
+        for c in range(chunks):
+            loads[1 + k * chunks + c].wait()
+            res[k, c] = low[k, c].astype(F32)
+            put(res.at[k, c], dst.at[c])
     loads[0].wait()
     for q in range(4):
         wi[:, q * features : (q + 1) * features] = mv[0, q].astype(F32)
         wo[q * share : (q + 1) * share] = mv[1, q].astype(F32)
     put(wi, gwi_ref)
     put(wo, gwo_ref)
-    for k, dst in enumerate((out_ref, gin_ref)):
-        for c in range(chunks):
-            loads[1 + k * chunks + c].wait()
-            res[k, c] = low[k, c].astype(F32)
-            put(res.at[k, c], dst.at[c])
     lanes = gvec_in.shape[1]
     for r in range(3):
         gci_ref[r * lanes : (r + 1) * lanes] = gvec_in[r]
@@ -797,9 +804,15 @@
             jax.ShapeDtypeStruct((2, 4, share, features), BF16),
             jax.ShapeDtypeStruct((8, 128), F32),
         ),
-        in_specs=[anywhere] * 4 + [inside] * 6 + [anywhere] * 4,
+        in_specs=[anywhere] * 14,
         out_specs=(anywhere, anywhere, inside, inside),
         scratch_shapes=[
+            vm((4 * features,), F32),
+            vm((features,), F32),
+            vm((features,), F32),
+            vm((features,), F32),
+            vm((features,), F32),
+            vm((features,), F32),
             vm((features, features), BF16),
             vm((features, features), BF16),
             vm((period, period), BF16),
@@ -832,7 +845,7 @@
             vm((8, 8, 128), F32),
             vm((8, 128), F32),
             vm((3, 8, 128), F32),
-            dma((4,)),
+            dma((10,)),
             dma((CHUNKS,)),
             dma((CHUNKS,)),
             dma((4,)),

time: 148 us -> 147 us (level)
  Pallas kernels: 147 us -> 145 us
where the time goes in v1:
time: 147 us; the launch traced here: 146 us
  Pallas kernels  145 us (99%)
    pallas_call x1, Pallas kernels, exchange_body(): pl.pallas_call(layer_kernel, out_shape=(jax.ShapeDtypeStruct(whole, BF16)...  140 us
    pallas_call x1, Pallas kernels, exchange_body(): pl.pallas_call(finish_kernel, in_specs=[anywhere] * 3 + [inside], out_spe...  5.35 us

profile of v1, /device:TPU:0, one launch (start us, length us, event | category | flops | bytes accessed | tf_op | source)
XLA Modules:
  0.0 146.2 jit_solution(9837781853957942016)
XLA Ops:
  0.6 140.0 %shard_map.213 = (bf16[3,256,768]{2,1,0:T(8,128)(2,1)}, bf16[3,256,768]{2,1,0:T(8,128)(2,1)}, bf16[2,4,96,768]{3,2,1,0:T(8,128)(2,1)}, f32[8,128]{1,0:T(8,128)}) custom-call(f32[3,256,768]{2,1,0:T(8,128)} %bitcast.12, f32[3,256,768]{2,1,0:T(8,128)} %bitcast.13, f32[768,3072]{1,0:T(8,128)} %win_hbm.1, f32[3072,768]{1,0:T(8,128)} %wout_hbm.1, f32[3072]{0:T(1024)} %cin_hbm.1, ...), custom_call_target="tpu_custom_call" | custom-call | tf_op jit(solution)/shard_map/pallas_call | solution.py:799
  140.7 5.3 %shard_map.214 = (f32[3,256,768]{2,1,0:T(8,128)}, f32[3,256,768]{2,1,0:T(8,128)}, f32[96,3072]{1,0:T(8,128)}, f32[384,768]{1,0:T(8,128)}, f32[384]{0:T(512)}, /*...) custom-call(bf16[3,256,768]{2,1,0:T(8,128)(2,1)} %get-tuple-element.24.out_in, ...), custom_call_target="tpu_custom_call" | custom-call | tf_op jit(solution)/shard_map/pallas_call | solution.py:872

commit v2 on v1

--- a/solution.py
+++ b/solution.py
@@ -637,10 +637,6 @@
             send_back(0, 1)
             owners_sent(0, 2)
 
-        @pl.when(c == 1)
-        def _():
-            send_owners(1, 0)
-
         feed_mid(c)
 
         @pl.when(c == 0)
@@ -660,6 +656,10 @@
             hop(3, 0)
 
         feed_end(c)
+
+        @pl.when(c == 0)
+        def _():
+            send_owners(1, 0)
 
         @pl.when(c == 1)
         def _():

time: 147 us -> 147 us (level)
  no operation moved by 1% of the time
where the time goes in v2:
time: 147 us; the launch traced here: 146 us
  Pallas kernels  146 us (99%)
    pallas_call x1, Pallas kernels, exchange_body(): pl.pallas_call(layer_kernel, out_shape=(jax.ShapeDtypeStruct(whole, BF16)...  140 us
    pallas_call x1, Pallas kernels, exchange_body(): pl.pallas_call(finish_kernel, in_specs=[anywhere] * 3 + [inside], out_spe...  5.35 us

profile of v2, /device:TPU:0, one launch (start us, length us, event | category | flops | bytes accessed | tf_op | source)
XLA Modules:
  0.0 146.4 jit_solution(11808341565340945183)
XLA Ops:
  0.6 140.2 %shard_map.213 = (bf16[3,256,768]{2,1,0:T(8,128)(2,1)}, bf16[3,256,768]{2,1,0:T(8,128)(2,1)}, bf16[2,4,96,768]{3,2,1,0:T(8,128)(2,1)}, f32[8,128]{1,0:T(8,128)}) custom-call(f32[3,256,768]{2,1,0:T(8,128)} %bitcast.12, f32[3,256,768]{2,1,0:T(8,128)} %bitcast.13, f32[768,3072]{1,0:T(8,128)} %win_hbm.1, f32[3072,768]{1,0:T(8,128)} %wout_hbm.1, f32[3072]{0:T(1024)} %cin_hbm.1, ...), custom_call_target="tpu_custom_call" | custom-call | tf_op jit(solution)/shard_map/pallas_call | solution.py:799
  140.9 5.3 %shard_map.214 = (f32[3,256,768]{2,1,0:T(8,128)}, f32[3,256,768]{2,1,0:T(8,128)}, f32[96,3072]{1,0:T(8,128)}, f32[384,768]{1,0:T(8,128)}, f32[384]{0:T(512)}, /*...) custom-call(bf16[3,256,768]{2,1,0:T(8,128)(2,1)} %get-tuple-element.24.out_in, ...), custom_call_target="tpu_custom_call" | custom-call | tf_op jit(solution)/shard_map/pallas_call | solution.py:872
